TPU v7x, 32 devices: a whole 2x2x4 slice. The times are simulated.
32 devices in a mesh: seq: 8 (over z, x), chan: 4 (over y, core).
Axes of the slice: x: 2, y: 2, z: 4, core: 2. Of those that a mesh axis runs over, the one named last changes fastest.
Arguments:
- signal: bfloat16 [2048, 1024], P('chan', 'seq'), may hold values from -6 to 6
- filters: float32 [2048, 1024], P('chan', 'seq'), may hold values from -1 to 1
- skip: float32 [2048], P('chan'), may hold values from 0.5 to 2
- weight: bfloat16 [2048, 8192], P(None, 'chan'), may hold values from -0.125 to 0.125
Outputs:
- mixed: bfloat16 [1024, 8192], P('seq', 'chan')
All inputs are finite; a program needn't handle non-finite values.
Results may differ from a plain program's by a relative error of at most 0.0049.
Values may be sent and summed in bfloat16 or wider, within the bound.
A program may use at most 128 MiB of HBM per device.

v0:
```python
import functools

import jax
import jax.numpy as jnp
from jax import lax
from jax.experimental import pallas as pl
from jax.experimental.pallas import tpu as pltpu
from jax.sharding import PartitionSpec as P

MESH = pl.DeviceIdType.MESH
VMEM = pl.BlockSpec(memory_space=pltpu.VMEM)
PARTS = 2
SHARE = 4
LIMIT = 64 * 1024 * 1024


def greet(peers):
    barrier = pltpu.get_barrier_semaphore()
    for peer in peers:
        pl.semaphore_signal(barrier, inc=1, device_id=peer, device_id_type=MESH)
    pl.semaphore_wait(barrier, len(peers))


class Toeplitz:
    def __init__(self, groups, tokens, width):
        self.groups, self.tokens = groups, tokens
        self.width, self.count = width, tokens // width
        row = lax.broadcasted_iota(jnp.int32, (width, tokens), 0)
        lane = lax.broadcasted_iota(jnp.int32, (width, tokens), 1)
        self.inside = lax.rem(lane, width) < width - row
        self.lane = lax.broadcasted_iota(jnp.int32, (groups, tokens), 1)
        self.piece = self.lane // width
        self.row = lax.broadcasted_iota(jnp.int32, (groups, tokens), 0)

    def turn(self, value, pieces):
        pieces = pieces % self.count
        return pltpu.roll(value, pieces * self.width, 1) if pieces else value

    def gather(self, pick):
        value = pick(0)
        for p in range(1, self.count):
            value = jnp.where(self.piece == p, pick(p), value)
        return value

    def down(self, value):
        return jnp.where(self.row >= 1, pltpu.roll(value, 1, 0), 0.0)

    def matrix(self, taps):
        count, width, tokens = self.count, self.width, self.tokens
        here = [
            self.gather(lambda g, e=e: self.turn(taps[g], g - e)) for e in range(count)
        ]
        following = [self.turn(value, -1) for value in here]
        before = [self.down(following[-1])] + following[:-1]
        parts = []
        for d in range(self.groups):
            for e in reversed(range(count)):
                near = jnp.broadcast_to(here[e][d : d + 1, :], (width, tokens))
                far = jnp.broadcast_to(before[e][d : d + 1, :], (width, tokens))
                tile = pltpu.roll(
                    jnp.where(self.inside, near, far), 0, 1, stride=1, stride_axis=0
                )
                parts.append(tile.astype(jnp.bfloat16))
        return jnp.concatenate(parts, axis=0)

    def windows(self, value):
        previous = self.down(value)
        views = []
        for b in range(self.count):
            back = self.count - 1 - b
            kept = jnp.where(self.piece < self.count - back, value, previous)
            views.append(self.turn(kept, back))
        return views


def layer_kernel(
    groups, lanes, parts, signal_ref, filter_ref, skip_ref, weight_ref, out_ref,
    raw, cast, gains, recv, source, taps, result, padded, values, gathered, held, left, total,
    load_sem, split_send, split_recv, seq_send, seq_recv,
    chan_send, chan_recv, pass_send, pass_recv,
):
    me = lax.axis_index("seq")
    lane = lax.axis_index("chan")
    tokens = signal_ref.shape[1]
    own = signal_ref.shape[0] // groups
    part = own // parts
    sibling = lane + 1 - 2 * lax.rem(lane, 2)
    others = [lax.rem(lane + 2 * j, lanes) for j in range(1, lanes // 2)]
    partners = [lax.rem(me + k, groups) for k in range(1, groups)]

    filter_load = pltpu.make_async_copy(filter_ref, raw, load_sem.at[0])
    skip_load = pltpu.make_async_copy(skip_ref, gains, load_sem.at[1])
    weight_load = pltpu.make_async_copy(weight_ref, held, load_sem.at[2])
    own_loads = [
        pltpu.make_async_copy(
            signal_ref.at[pl.ds(me * own + h * part, part)], recv.at[h, 0, 0], load_sem.at[3 + h]
        )
        for h in range(parts)
    ]
    filter_load.start()
    for load in own_loads:
        load.start()
    skip_load.start()
    greet(
        [{"seq": peer} for peer in partners]
        + [{"chan": other} for other in others]
        + [{"chan": sibling}]
    )
    sent = []

    def push(origin, target, send_sem, recv_sem, device):
        copy = pltpu.make_async_remote_copy(
            src_ref=origin,
            dst_ref=target,
            send_sem=send_sem,
            recv_sem=recv_sem,
            device_id=device,
            device_id_type=MESH,
        )
        copy.start()
        sent.append(copy)
        return copy

    def split(h, which, origin):
        return [
            push(
                origin.at[pl.ds(peer * own + h * part, part)],
                recv.at[h, k + 1, which],
                split_send.at[h, which, k],
                split_recv.at[h, which, k],
                {"seq": peer},
            )
            for k, peer in enumerate(partners)
        ]

    tools = Toeplitz(groups, tokens, tokens // SHARE)

    def unpack(h):
        for k in range(groups):
            place = lax.rem(me - k + groups, groups)
            rows = pl.ds(pl.multiple_of(place * part, part), part)
            source[rows, :] = recv[h, k, 0].astype(jnp.float32)
            taps[rows, :] = recv[h, k, 1].astype(jnp.float32)

    def convolve(h, begin, end):
        def several(step, carry):
            first = step * SHARE
            picks = [pl.ds(first + g, groups, stride=part) for g in range(SHARE)]
            inputs = [source[pick, :] for pick in picks]
            for g in range(SHARE):
                for b, view in enumerate(tools.windows(inputs[g])):
                    padded[g * SHARE + b, groups:, :] = view
            rows = jnp.concatenate(
                [
                    padded[:, groups - d : 2 * groups - d, :]
                    .reshape(SHARE * SHARE * groups, tokens)
                    .astype(jnp.bfloat16)
                    for d in range(groups)
                ],
                axis=1,
            )
            columns = tools.matrix([taps[pick, :] for pick in picks])
            both = jnp.dot(rows, columns, preferred_element_type=jnp.float32)
            both = both.reshape(SHARE, SHARE, groups, tokens)
            base = me * own + h * part + first
            for g, pick in enumerate(picks):
                joined = tools.gather(lambda b, g=g: tools.turn(both[g, b], b - g))
                result[pick, :] = joined + gains[base + g] * inputs[g]
            return carry

        lax.fori_loop(begin, end, several, 0)

    def pack(h):
        for k in range(groups):
            values[h, k] = result[k * part : (k + 1) * part, :].astype(values.dtype)

    def slot(h, which, at):
        return gathered.at[h, which, at]

    def send_values(h):
        copies = [
            push(
                values.at[h, peer], slot(h, lane, me), seq_send.at[h, k], seq_recv.at[h, k],
                {"seq": peer},
            )
            for k, peer in enumerate(partners)
        ]
        gathered[h, lane, me] = values[h, me]
        return copies

    def spread(h, arrivals):
        crossing, inside = [], []
        for k in range(groups):
            at = lax.rem(me - k + groups, groups)
            if k:
                arrivals[k - 1].wait_recv()
            for j, other in enumerate(others):
                crossing.append((j, k, push(
                    slot(h, lane, at), slot(h, lane, at),
                    chan_send.at[h, j, k], chan_recv.at[h, j, k], {"chan": other},
                )))
            inside.append(push(
                slot(h, lane, at), slot(h, lane, at),
                pass_send.at[h, 0, k], pass_recv.at[h, 0, k], {"chan": sibling},
            ))
        return crossing, inside

    def hand_over(h, crossing, inside):
        for j, k, copy in crossing:
            copy.wait_recv()
            at = lax.rem(me - k + groups, groups)
            origin = lax.rem(lane - 2 * (j + 1) + lanes, lanes)
            inside.append(push(
                slot(h, origin, at), slot(h, origin, at),
                pass_send.at[h, j + 1, k], pass_recv.at[h, j + 1, k], {"chan": sibling},
            ))

    wide = 512 if out_ref.shape[1] % 512 == 0 else out_ref.shape[1]
    tiles = out_ref.shape[1] // wide
    depth = lanes * groups * part

    def settle(h, inside):
        for copy in inside:
            copy.wait_recv()
        left[...] = gathered[h].reshape(depth, tokens).T

    def project(h, begin, end):
        def tile(step, carry):
            columns = pl.ds(pl.multiple_of(step * wide, wide), wide)
            block = held[:, h * part : (h + 1) * part, columns].reshape(depth, wide)
            amount = jnp.dot(left[...], block, preferred_element_type=jnp.float32)
            if h:
                amount = amount + total[:, columns]
            if h == parts - 1:
                out_ref[:, columns] = amount.astype(out_ref.dtype)
            else:
                total[:, columns] = amount
            return carry

        lax.fori_loop(begin, end, tile, 0)

    incoming = [split(0, 0, signal_ref)]
    filter_load.wait()
    cast[...] = raw[...].astype(cast.dtype)
    incoming.append(split(0, 1, cast))
    for h in range(parts):
        recv[h, 0, 1] = cast[pl.ds(me * own + h * part, part), :]
    skip_load.wait()
    padded[:, :groups, :] = jnp.zeros((SHARE * SHARE, groups, tokens), jnp.float32)
    weight_load.start()
    turns = part // SHARE
    arrivals = crossing = inside = None
    for h in range(parts):
        own_loads[h].wait()
        for copies in incoming:
            for copy in copies:
                copy.wait_recv()
        if h + 1 < parts:
            incoming = [split(h + 1, 0, signal_ref), split(h + 1, 1, cast)]
        unpack(h)
        if h:
            convolve(h, 0, turns // 2)
            crossing, inside = spread(h - 1, arrivals)
            convolve(h, turns // 2, turns)
            hand_over(h - 1, crossing, inside)
        else:
            convolve(h, 0, turns)
        pack(h)
        arrivals = send_values(h)
        if h == 1:
            weight_load.wait()
        if h:
            settle(h - 1, inside)
            project(h - 1, 0, tiles // 2)
    last = parts - 1
    crossing, inside = spread(last, arrivals)
    if last:
        project(last - 1, tiles // 2, tiles)
    else:
        weight_load.wait()
    hand_over(last, crossing, inside)
    settle(last, inside)
    project(last, 0, tiles)
    for copy in sent:
        copy.wait_send()


def per_device(signal, filters, skip, weight):
    groups = lax.axis_size("seq")
    lanes = lax.axis_size("chan")
    channels, tokens = signal.shape
    features = weight.shape[1]
    own = channels // groups
    parts = PARTS if own % (16 * PARTS) == 0 else 1
    part = own // parts
    across = max(lanes // 2 - 1, 1)
    half, full = jnp.bfloat16, jnp.float32
    dma = pltpu.SemaphoreType.DMA
    whole = pl.BlockSpec(memory_space=pltpu.HBM)
    return pl.pallas_call(
        functools.partial(layer_kernel, groups, lanes, parts),
        out_shape=jax.ShapeDtypeStruct((tokens, features), half),
        in_specs=[whole] * 4,
        out_specs=VMEM,
        scratch_shapes=[
            pltpu.VMEM((channels, tokens), full),
            pltpu.VMEM((channels, tokens), half),
            pltpu.SMEM((channels,), full),
            pltpu.VMEM((parts, groups, 2, part, tokens), half),
            pltpu.VMEM((groups * part, tokens), full),
            pltpu.VMEM((groups * part, tokens), full),
            pltpu.VMEM((groups * part, tokens), full),
            pltpu.VMEM((SHARE * SHARE, 2 * groups, tokens), full),
            pltpu.VMEM((parts, groups, part, tokens), half),
            pltpu.VMEM((parts, lanes, groups, part, tokens), half),
            pltpu.VMEM((lanes * groups, own, features), half),
            pltpu.VMEM((tokens, lanes * groups * part), half),
            pltpu.VMEM((tokens, features), full),
            dma((3 + parts,)),
            dma((parts, 2, groups - 1)),
            dma((parts, 2, groups - 1)),
            dma((parts, groups - 1)),
            dma((parts, groups - 1)),
            dma((parts, across, groups)),
            dma((parts, across, groups)),
            dma((parts, lanes // 2, groups)),
            dma((parts, lanes // 2, groups)),
        ],
        compiler_params=pltpu.CompilerParams(
            collective_id=0, has_side_effects=True, vmem_limit_bytes=LIMIT
        ),
    )(signal, filters, skip, weight.reshape(lanes * groups, own, features))


def solution(mesh):
    in_specs = (P("chan", "seq"), P("chan", "seq"), P("chan"), P(None, "chan"))
    out_specs = P("seq", "chan")
    return jax.shard_map(
        per_device, mesh=mesh, in_specs=in_specs, out_specs=out_specs, check_vma=False
    )
```

profile of v0, /device:TPU:1, one launch (start us, length us, event | category | flops | bytes accessed | tf_op | source)
XLA Modules:
  0.0 35.1 jit_solution(15084495797565079254)
XLA Ops:
  0.0 33.2 %shard_map.46 = bf16[128,2048]{1,0:T(8,128)(2,1)} custom-call(bf16[512,128]{1,0:T(8,128)(2,1)} %signal_ref.1, f32[512,128]{1,0:T(8,128)} %filter_ref.1, f32[512]{0:T(512)} %skip_ref.1, bf16[32,64,2048]{2,1,0:T(8,128)(2,1)} %bitcast.1), custom_call_target="tpu_custom_call" | custom-call | tf_op jit(solution)/shard_map/pallas_call | solution.py:300
  33.3 1.9 %copy.6 = bf16[128,2048]{1,0:T(8,128)(2,1)} copy(bf16[128,2048]{1,0:T(8,128)(2,1)} %shard_map.46) | data formatting | bytes 1048576
where the time goes:
time: 35.3 us; the launch traced here: 35.1 us
  Pallas kernels  33.2 us (94%)
  local copies, waits for them, and re-layouts  1.88 us (5%)
    pallas_call x1, Pallas kernels, per_device(): pl.pallas_call(functools.partial(layer_kernel, groups, lanes, parts), out...  33.2 us
    unnamed x1, local copies, waits for them, and re-layouts  1.88 us

commit v1 on v0

--- a/solution.py
+++ b/solution.py
@@ -11,6 +11,7 @@
 VMEM = pl.BlockSpec(memory_space=pltpu.VMEM)
 PARTS = 2
 SHARE = 4
+ROOMS = 2
 LIMIT = 64 * 1024 * 1024
 
 
@@ -75,15 +76,14 @@
 
 def layer_kernel(
     groups, lanes, parts, signal_ref, filter_ref, skip_ref, weight_ref, out_ref,
-    raw, cast, gains, recv, source, taps, result, padded, values, gathered, held, left, total,
+    raw, stage, gains, recv, source, taps, result, padded, values, gathered, held, left, total,
     load_sem, split_send, split_recv, seq_send, seq_recv,
     chan_send, chan_recv, pass_send, pass_recv,
 ):
     me = lax.axis_index("seq")
     lane = lax.axis_index("chan")
-    tokens = signal_ref.shape[1]
-    own = signal_ref.shape[0] // groups
-    part = own // parts
+    part, tokens = signal_ref.shape[2:]
+    own = parts * part
     sibling = lane + 1 - 2 * lax.rem(lane, 2)
     others = [lax.rem(lane + 2 * j, lanes) for j in range(1, lanes // 2)]
     partners = [lax.rem(me + k, groups) for k in range(1, groups)]
@@ -91,14 +91,12 @@
     filter_load = pltpu.make_async_copy(filter_ref, raw, load_sem.at[0])
     skip_load = pltpu.make_async_copy(skip_ref, gains, load_sem.at[1])
     weight_load = pltpu.make_async_copy(weight_ref, held, load_sem.at[2])
-    own_loads = [
-        pltpu.make_async_copy(
-            signal_ref.at[pl.ds(me * own + h * part, part)], recv.at[h, 0, 0], load_sem.at[3 + h]
-        )
+    signal_loads = [
+        pltpu.make_async_copy(signal_ref.at[:, h], stage.at[h, :, 0], load_sem.at[3 + h])
         for h in range(parts)
     ]
     filter_load.start()
-    for load in own_loads:
+    for load in signal_loads:
         load.start()
     skip_load.start()
     greet(
@@ -121,13 +119,10 @@
         sent.append(copy)
         return copy
 
-    def split(h, which, origin):
+    def split(h):
         return [
             push(
-                origin.at[pl.ds(peer * own + h * part, part)],
-                recv.at[h, k + 1, which],
-                split_send.at[h, which, k],
-                split_recv.at[h, which, k],
+                stage.at[h, peer], recv.at[h, k + 1], split_send.at[h, k], split_recv.at[h, k],
                 {"seq": peer},
             )
             for k, peer in enumerate(partners)
@@ -143,16 +138,15 @@
             taps[rows, :] = recv[h, k, 1].astype(jnp.float32)
 
     def convolve(h, begin, end):
-        def several(step, carry):
-            first = step * SHARE
+        def several(first, room):
             picks = [pl.ds(first + g, groups, stride=part) for g in range(SHARE)]
             inputs = [source[pick, :] for pick in picks]
             for g in range(SHARE):
                 for b, view in enumerate(tools.windows(inputs[g])):
-                    padded[g * SHARE + b, groups:, :] = view
+                    padded[room, g * SHARE + b, groups:, :] = view
             rows = jnp.concatenate(
                 [
-                    padded[:, groups - d : 2 * groups - d, :]
+                    padded[room, :, groups - d : 2 * groups - d, :]
                     .reshape(SHARE * SHARE * groups, tokens)
                     .astype(jnp.bfloat16)
                     for d in range(groups)
@@ -163,12 +157,21 @@
             both = jnp.dot(rows, columns, preferred_element_type=jnp.float32)
             both = both.reshape(SHARE, SHARE, groups, tokens)
             base = me * own + h * part + first
-            for g, pick in enumerate(picks):
-                joined = tools.gather(lambda b, g=g: tools.turn(both[g, b], b - g))
-                result[pick, :] = joined + gains[base + g] * inputs[g]
+            return [
+                (pick, tools.gather(lambda b, g=g: tools.turn(both[g, b], b - g))
+                 + gains[base + g] * inputs[g])
+                for g, pick in enumerate(picks)
+            ]
+
+        def turn(step, carry):
+            done = []
+            for room in range(ROOMS):
+                done += several((step * ROOMS + room) * SHARE, room)
+            for pick, value in done:
+                result[pick, :] = value
             return carry
 
-        lax.fori_loop(begin, end, several, 0)
+        lax.fori_loop(begin, end, turn, 0)
 
     def pack(h):
         for k in range(groups):
@@ -188,31 +191,26 @@
         gathered[h, lane, me] = values[h, me]
         return copies
 
+    def hand(h, which, send_sem, recv_sem, device):
+        row = gathered.at[h, which]
+        return push(row, row, send_sem, recv_sem, device)
+
     def spread(h, arrivals):
-        crossing, inside = [], []
-        for k in range(groups):
-            at = lax.rem(me - k + groups, groups)
-            if k:
-                arrivals[k - 1].wait_recv()
-            for j, other in enumerate(others):
-                crossing.append((j, k, push(
-                    slot(h, lane, at), slot(h, lane, at),
-                    chan_send.at[h, j, k], chan_recv.at[h, j, k], {"chan": other},
-                )))
-            inside.append(push(
-                slot(h, lane, at), slot(h, lane, at),
-                pass_send.at[h, 0, k], pass_recv.at[h, 0, k], {"chan": sibling},
-            ))
+        for copy in arrivals:
+            copy.wait_recv()
+        crossing = [
+            hand(h, lane, chan_send.at[h, j], chan_recv.at[h, j], {"chan": other})
+            for j, other in enumerate(others)
+        ]
+        inside = [hand(h, lane, pass_send.at[h, 0], pass_recv.at[h, 0], {"chan": sibling})]
         return crossing, inside
 
     def hand_over(h, crossing, inside):
-        for j, k, copy in crossing:
+        for j, copy in enumerate(crossing):
             copy.wait_recv()
-            at = lax.rem(me - k + groups, groups)
             origin = lax.rem(lane - 2 * (j + 1) + lanes, lanes)
-            inside.append(push(
-                slot(h, origin, at), slot(h, origin, at),
-                pass_send.at[h, j + 1, k], pass_recv.at[h, j + 1, k], {"chan": sibling},
+            inside.append(hand(
+                h, origin, pass_send.at[h, j + 1], pass_recv.at[h, j + 1], {"chan": sibling}
             ))
 
     wide = 512 if out_ref.shape[1] % 512 == 0 else out_ref.shape[1]
@@ -239,24 +237,22 @@
 
         lax.fori_loop(begin, end, tile, 0)
 
-    incoming = [split(0, 0, signal_ref)]
     filter_load.wait()
-    cast[...] = raw[...].astype(cast.dtype)
-    incoming.append(split(0, 1, cast))
-    for h in range(parts):
-        recv[h, 0, 1] = cast[pl.ds(me * own + h * part, part), :]
+    stage[:, :, 1] = jnp.swapaxes(raw[...].astype(stage.dtype), 0, 1)
+    signal_loads[0].wait()
+    incoming = split(0)
     skip_load.wait()
-    padded[:, :groups, :] = jnp.zeros((SHARE * SHARE, groups, tokens), jnp.float32)
+    padded[:, :, :groups, :] = jnp.zeros((ROOMS, SHARE * SHARE, groups, tokens), jnp.float32)
     weight_load.start()
-    turns = part // SHARE
+    turns = part // (SHARE * ROOMS)
     arrivals = crossing = inside = None
     for h in range(parts):
-        own_loads[h].wait()
-        for copies in incoming:
-            for copy in copies:
-                copy.wait_recv()
+        recv[h, 0] = stage[h, me]
+        for copy in incoming:
+            copy.wait_recv()
         if h + 1 < parts:
-            incoming = [split(h + 1, 0, signal_ref), split(h + 1, 1, cast)]
+            signal_loads[h + 1].wait()
+            incoming = split(h + 1)
         unpack(h)
         if h:
             convolve(h, 0, turns // 2)
@@ -303,33 +299,38 @@
         in_specs=[whole] * 4,
         out_specs=VMEM,
         scratch_shapes=[
-            pltpu.VMEM((channels, tokens), full),
-            pltpu.VMEM((channels, tokens), half),
+            pltpu.VMEM((groups, parts, part, tokens), full),
+            pltpu.VMEM((parts, groups, 2, part, tokens), half),
             pltpu.SMEM((channels,), full),
             pltpu.VMEM((parts, groups, 2, part, tokens), half),
             pltpu.VMEM((groups * part, tokens), full),
             pltpu.VMEM((groups * part, tokens), full),
             pltpu.VMEM((groups * part, tokens), full),
-            pltpu.VMEM((SHARE * SHARE, 2 * groups, tokens), full),
+            pltpu.VMEM((ROOMS, SHARE * SHARE, 2 * groups, tokens), full),
             pltpu.VMEM((parts, groups, part, tokens), half),
             pltpu.VMEM((parts, lanes, groups, part, tokens), half),
             pltpu.VMEM((lanes * groups, own, features), half),
             pltpu.VMEM((tokens, lanes * groups * part), half),
             pltpu.VMEM((tokens, features), full),
             dma((3 + parts,)),
-            dma((parts, 2, groups - 1)),
-            dma((parts, 2, groups - 1)),
             dma((parts, groups - 1)),
             dma((parts, groups - 1)),
-            dma((parts, across, groups)),
-            dma((parts, across, groups)),
-            dma((parts, lanes // 2, groups)),
-            dma((parts, lanes // 2, groups)),
+            dma((parts, groups - 1)),
+            dma((parts, groups - 1)),
+            dma((parts, across)),
+            dma((parts, across)),
+            dma((parts, lanes // 2)),
+            dma((parts, lanes // 2)),
         ],
         compiler_params=pltpu.CompilerParams(
             collective_id=0, has_side_effects=True, vmem_limit_bytes=LIMIT
         ),
-    )(signal, filters, skip, weight.reshape(lanes * groups, own, features))
+    )(
+        signal.reshape(groups, parts, part, tokens),
+        filters.reshape(groups, parts, part, tokens),
+        skip,
+        weight.reshape(lanes * groups, own, features),
+    )
 
 
 def solution(mesh):

time: 35.3 us -> 32.9 us (0.932)
  Pallas kernels: 33.2 us -> 30.8 us
    pallas_call x1, Pallas kernels: 33.2 us -> 30.8 us  [per_device(): pl.pallas_call(functools.partial(layer_kernel, groups, lanes, parts), out...]
where the time goes in v1:
time: 32.9 us; the launch traced here: 32.7 us
  Pallas kernels  30.8 us (94%)
  local copies, waits for them, and re-layouts  1.88 us (6%)
    pallas_call x1, Pallas kernels, per_device(): pl.pallas_call(functools.partial(layer_kernel, groups, lanes, parts), out...  30.8 us
    unnamed x1, local copies, waits for them, and re-layouts  1.88 us

profile of v1, /device:TPU:1, one launch (start us, length us, event | category | flops | bytes accessed | tf_op | source)
XLA Modules:
  0.0 32.7 jit_solution(9945212039629895550)
XLA Ops:
  0.0 30.8 %shard_map.46 = bf16[128,2048]{1,0:T(8,128)(2,1)} custom-call(bf16[8,2,32,128]{3,2,1,0:T(8,128)(2,1)} %bitcast.5, f32[8,2,32,128]{3,2,1,0:T(8,128)} %bitcast.4, f32[512]{0:T(512)} %skip_ref.1, bf16[32,64,2048]{2,1,0:T(8,128)(2,1)} %bitcast.3), custom_call_target="tpu_custom_call" | custom-call | tf_op jit(solution)/shard_map/pallas_call | solution.py:296
  30.8 1.9 %copy.6 = bf16[128,2048]{1,0:T(8,128)(2,1)} copy(bf16[128,2048]{1,0:T(8,128)(2,1)} %shard_map.46) | data formatting | bytes 1048576

commit v2 on v1

--- a/solution.py
+++ b/solution.py
@@ -9,7 +9,7 @@
 
 MESH = pl.DeviceIdType.MESH
 VMEM = pl.BlockSpec(memory_space=pltpu.VMEM)
-PARTS = 2
+PARTS = 4
 SHARE = 4
 ROOMS = 2
 LIMIT = 64 * 1024 * 1024
@@ -78,14 +78,13 @@
     groups, lanes, parts, signal_ref, filter_ref, skip_ref, weight_ref, out_ref,
     raw, stage, gains, recv, source, taps, result, padded, values, gathered, held, left, total,
     load_sem, split_send, split_recv, seq_send, seq_recv,
-    chan_send, chan_recv, pass_send, pass_recv,
+    chan_send, chan_recv,
 ):
     me = lax.axis_index("seq")
     lane = lax.axis_index("chan")
     part, tokens = signal_ref.shape[2:]
     own = parts * part
-    sibling = lane + 1 - 2 * lax.rem(lane, 2)
-    others = [lax.rem(lane + 2 * j, lanes) for j in range(1, lanes // 2)]
+    others = [lax.rem(lane + j, lanes) for j in range(1, lanes)]
     partners = [lax.rem(me + k, groups) for k in range(1, groups)]
 
     filter_load = pltpu.make_async_copy(filter_ref, raw, load_sem.at[0])
@@ -102,7 +101,6 @@
     greet(
         [{"seq": peer} for peer in partners]
         + [{"chan": other} for other in others]
-        + [{"chan": sibling}]
     )
     sent = []
 
@@ -198,20 +196,11 @@
     def spread(h, arrivals):
         for copy in arrivals:
             copy.wait_recv()
-        crossing = [
-            hand(h, lane, chan_send.at[h, j], chan_recv.at[h, j], {"chan": other})
+        row = gathered.at[h, lane]
+        return [
+            push(row, row, chan_send.at[h, j], chan_recv.at[h, j], {"chan": other})
             for j, other in enumerate(others)
         ]
-        inside = [hand(h, lane, pass_send.at[h, 0], pass_recv.at[h, 0], {"chan": sibling})]
-        return crossing, inside
-
-    def hand_over(h, crossing, inside):
-        for j, copy in enumerate(crossing):
-            copy.wait_recv()
-            origin = lax.rem(lane - 2 * (j + 1) + lanes, lanes)
-            inside.append(hand(
-                h, origin, pass_send.at[h, j + 1], pass_recv.at[h, j + 1], {"chan": sibling}
-            ))
 
     wide = 512 if out_ref.shape[1] % 512 == 0 else out_ref.shape[1]
     tiles = out_ref.shape[1] // wide
@@ -240,42 +229,44 @@
     filter_load.wait()
     stage[:, :, 1] = jnp.swapaxes(raw[...].astype(stage.dtype), 0, 1)
     signal_loads[0].wait()
-    incoming = split(0)
+    incoming = [split(0)]
     skip_load.wait()
     padded[:, :, :groups, :] = jnp.zeros((ROOMS, SHARE * SHARE, groups, tokens), jnp.float32)
+    if parts > 1:
+        signal_loads[1].wait()
+        incoming.append(split(1))
     weight_load.start()
     turns = part // (SHARE * ROOMS)
-    arrivals = crossing = inside = None
+    arrivals, inside = [], []
     for h in range(parts):
         recv[h, 0] = stage[h, me]
-        for copy in incoming:
+        for copy in incoming[h]:
             copy.wait_recv()
-        if h + 1 < parts:
-            signal_loads[h + 1].wait()
-            incoming = split(h + 1)
+        if h + 2 < parts:
+            signal_loads[h + 2].wait()
+            incoming.append(split(h + 2))
         unpack(h)
-        if h:
-            convolve(h, 0, turns // 2)
-            crossing, inside = spread(h - 1, arrivals)
-            convolve(h, turns // 2, turns)
-            hand_over(h - 1, crossing, inside)
-        else:
-            convolve(h, 0, turns)
+        convolve(h, 0, turns)
         pack(h)
-        arrivals = send_values(h)
+        arrivals.append(send_values(h))
         if h == 1:
             weight_load.wait()
-        if h:
-            settle(h - 1, inside)
-            project(h - 1, 0, tiles // 2)
+        if h >= 1:
+            inside.append(spread(h - 1, arrivals[h - 1]))
+        if h >= 2 and h < parts - 1:
+            settle(h - 2, inside[h - 2])
+            project(h - 2, 0, tiles)
     last = parts - 1
-    crossing, inside = spread(last, arrivals)
-    if last:
-        project(last - 1, tiles // 2, tiles)
-    else:
+    if last == 0:
         weight_load.wait()
-    hand_over(last, crossing, inside)
-    settle(last, inside)
+    if last >= 2:
+        settle(last - 2, inside[last - 2])
+        project(last - 2, 0, tiles)
+    inside.append(spread(last, arrivals[last]))
+    if last >= 1:
+        settle(last - 1, inside[last - 1])
+        project(last - 1, 0, tiles)
+    settle(last, inside[last])
     project(last, 0, tiles)
     for copy in sent:
         copy.wait_send()
@@ -289,13 +280,12 @@
     own = channels // groups
     parts = PARTS if own % (16 * PARTS) == 0 else 1
     part = own // parts
-    across = max(lanes // 2 - 1, 1)
     half, full = jnp.bfloat16, jnp.float32
     dma = pltpu.SemaphoreType.DMA
     whole = pl.BlockSpec(memory_space=pltpu.HBM)
-    return pl.pallas_call(
+    sums = pl.pallas_call(
         functools.partial(layer_kernel, groups, lanes, parts),
-        out_shape=jax.ShapeDtypeStruct((tokens, features), half),
+        out_shape=jax.ShapeDtypeStruct((tokens, features), full),
         in_specs=[whole] * 4,
         out_specs=VMEM,
         scratch_shapes=[
@@ -317,10 +307,8 @@
             dma((parts, groups - 1)),
             dma((parts, groups - 1)),
             dma((parts, groups - 1)),
-            dma((parts, across)),
-            dma((parts, across)),
-            dma((parts, lanes // 2)),
-            dma((parts, lanes // 2)),
+            dma((parts, lanes - 1)),
+            dma((parts, lanes - 1)),
         ],
         compiler_params=pltpu.CompilerParams(
             collective_id=0, has_side_effects=True, vmem_limit_bytes=LIMIT
@@ -331,6 +319,7 @@
         skip,
         weight.reshape(lanes * groups, own, features),
     )
+    return sums.astype(half)
 
 
 def solution(mesh):

time: 32.9 us -> 32.8 us (level)
  other arithmetic: 0 us -> 2.09 us
  local copies, waits for them, and re-layouts: 1.88 us -> 0 us
  Pallas kernels: 30.8 us -> 30.3 us
    convert_element_type x0 -> x1, other arithmetic: none -> 2.09 us  [per_device(): return sums.astype(half)]
    unnamed x1 -> x0, local copies, waits for them, and re-layouts: 1.88 us -> none
    pallas_call x1, Pallas kernels: 30.8 us -> 30.3 us  [per_device(): pl.pallas_call(functools.partial(layer_kernel, groups, lanes, parts), out...]
where the time goes in v2:
time: 32.8 us; the launch traced here: 32.4 us
  Pallas kernels  30.3 us (92%)
  other arithmetic  2.09 us (6%)
    pallas_call x1, Pallas kernels, per_device(): pl.pallas_call(functools.partial(layer_kernel, groups, lanes, parts), out...  30.3 us
    convert_element_type x1, other arithmetic, per_device(): return sums.astype(half)  2.09 us

profile of v2, /device:TPU:1, one launch (start us, length us, event | category | flops | bytes accessed | tf_op | source)
XLA Modules:
  0.0 32.4 jit_solution(6657665883445366614)
XLA Ops:
  0.0 30.3 %shard_map.46 = f32[128,2048]{1,0:T(8,128)} custom-call(bf16[8,4,16,128]{3,2,1,0:T(8,128)(2,1)} %bitcast.5, f32[8,4,16,128]{3,2,1,0:T(8,128)} %bitcast.4, f32[512]{0:T(512)} %skip_ref.1, bf16[32,64,2048]{2,1,0:T(8,128)(2,1)} %bitcast.3), custom_call_target="tpu_custom_call" | custom-call | tf_op jit(solution)/shard_map/pallas_call | solution.py:286
  30.3 2.1 %convert_element_type.3 = bf16[128,2048]{1,0:T(8,128)(2,1)} convert(f32[128,2048]{1,0:T(8,128)} %shard_map.46) | non-fusion elementwise | flops 262144 | bytes 1572864 | tf_op jit(solution)/shard_map/convert_element_type | solution.py:322
